TPU v7x, 512 devices: a whole 4x8x8 slice. The times are simulated.
512 devices in a mesh: dp: 32 (over z, x_hi, core), tensor: 16 (over x_lo, y).
Axes of the slice: x: 4 (x_hi: 2, x_lo: 2; x = x_hi * 2 + x_lo), y: 8, z: 8, core: 2. Of those that a mesh axis runs over, the one named last changes fastest.
Arguments:
- gate_pre: bfloat16 [4096, 14336], P('dp', 'tensor'), may hold values from -6 to 6
- up_pre: bfloat16 [4096, 14336], P('dp', 'tensor'), may hold values from -6 to 6
- cotangent: bfloat16 [4096, 4096], P('dp', 'tensor'), may hold values from -6 to 6
- weight_tiles: bfloat16 [16, 96, 128, 128], P('tensor', 'dp'), may hold values from -0.109375 to 0.109375
- tile_slots: int32 [16, 96], P('tensor', 'dp'), may hold values from 0 to 223, as said below
- live_counts: int32 [16], P('tensor'), may hold values from 24 to 96, as said below
Outputs:
- projected: bfloat16 [4096, 4096], P('dp', 'tensor')
- gate_grad: bfloat16 [4096, 14336], P('dp', 'tensor')
- up_grad: bfloat16 [4096, 14336], P('dp', 'tensor')
- tile_grad: float32 [16, 96, 128, 128], P('tensor', 'dp')
Inputs may be any that keep to these rules, and one draw needn't show every extreme that they name: `tile_slots`: within one tensor shard all 96 entries are distinct. `live_counts`: some shard has all 96 slots live.
All inputs are finite; a program needn't handle non-finite values.
Results may differ from a plain program's by a relative error of at most 0.019.
Values may be sent and summed in bfloat16 or wider, within the bound.
A program may use at most 64 MiB of HBM per device.

v0:
```python
import jax
import jax.numpy as jnp
from jax import lax
from jax.sharding import PartitionSpec as P


def per_device(gate_pre, up_pre, cotangent, weight_tiles, tile_slots, live_counts):
    tok_rows = gate_pre.shape[0]
    hid_width = gate_pre.shape[1]
    tile_edge = weight_tiles.shape[2]
    hid_blocks = hid_width // tile_edge
    shards = lax.axis_size("tensor")
    local_blocks = cotangent.shape[1] // tile_edge
    model_blocks = local_blocks * shards
    token_scale = (tok_rows * lax.axis_size("dp")) ** (-0.5)
    group_size = 16
    gate_val = gate_pre.astype(jnp.float32)
    up_val = up_pre.astype(jnp.float32)
    gate_sig = jax.nn.sigmoid(gate_val)
    silu_val = gate_val * gate_sig
    hidden = (silu_val * up_val).astype(jnp.bfloat16)
    hidden_blocks = hidden.reshape(tok_rows, hid_blocks, tile_edge).transpose(1, 0, 2)
    fetched_tiles, fetched_slots = (
        lax.all_gather(weight_tiles, "dp", axis=1, tiled=True),
        lax.all_gather(tile_slots, "dp", axis=1, tiled=True),
    )
    all_tiles = fetched_tiles[0]
    all_slots = fetched_slots[0]
    capacity = all_tiles.shape[0]
    live_count = live_counts[0]
    groups = capacity // group_size

    def forward_group(group_index, totals):
        offset = group_index * group_size
        group_tiles = lax.dynamic_slice_in_dim(all_tiles, offset, group_size, 0)
        group_slots = lax.dynamic_slice_in_dim(all_slots, offset, group_size, 0)
        is_live = offset + jnp.arange(group_size, dtype=jnp.int32) < live_count
        hid_index = group_slots // model_blocks
        mod_index = group_slots % model_blocks
        picked = hidden_blocks[hid_index]
        product = jnp.einsum(
            "gtb,gbc->gtc", picked, group_tiles, preferred_element_type=jnp.float32
        )
        product = jnp.where(is_live[:, None, None], product, 0.0)
        return totals.at[mod_index].add(product)

    sums = lax.fori_loop(
        0, groups, forward_group, jnp.zeros((model_blocks, tok_rows, tile_edge), jnp.float32)
    )
    shared = sums.astype(jnp.bfloat16).reshape(1, model_blocks, tok_rows, tile_edge)
    received = lax.all_to_all(shared, "tensor", split_axis=1, concat_axis=0, tiled=True)
    column_total = jnp.sum(received.astype(jnp.float32), axis=0)
    projected = (
        column_total.transpose(1, 0, 2)
        .reshape(tok_rows, local_blocks * tile_edge)
        .astype(jnp.bfloat16)
    )
    cot_local = cotangent.reshape(tok_rows, local_blocks, tile_edge).transpose(1, 0, 2)
    all_cot = lax.all_gather(cot_local, "tensor", axis=0, tiled=True)
    part_tiles = lax.all_gather(weight_tiles, "dp", axis=1, tiled=True)[0]
    part_slots = lax.all_gather(tile_slots, "dp", axis=1, tiled=True)[0]
    hidden_grad = jnp.zeros((hid_blocks, tok_rows, tile_edge), jnp.float32)
    grad_buffer = jnp.zeros((capacity, tile_edge, tile_edge), jnp.float32)
    count_here = part_tiles.shape[0]
    is_live = jnp.arange(count_here, dtype=jnp.int32) < live_count
    hid_index = part_slots // model_blocks
    mod_index = part_slots % model_blocks
    picked = hidden_blocks[hid_index]
    cot_picked = all_cot[mod_index]
    back = jnp.einsum("gtc,gbc->gtb", cot_picked, part_tiles, preferred_element_type=jnp.float32)
    back = jnp.where(is_live[:, None, None], back, 0.0)
    hidden_grad = hidden_grad.at[hid_index].add(back)
    tile_terms = (
        jnp.einsum("gtb,gtc->gbc", picked, cot_picked, preferred_element_type=jnp.float32)
        * token_scale
    )
    tile_terms = jnp.where(is_live[:, None, None], tile_terms, 0.0)
    grad_buffer = lax.dynamic_update_slice_in_dim(grad_buffer, tile_terms, jnp.int32(0), 0)
    hidden_grad, grad_buffer = (hidden_grad, grad_buffer)
    tile_grad = lax.psum_scatter(
        grad_buffer.reshape(1, capacity, tile_edge, tile_edge).astype(jnp.bfloat16),
        "dp",
        scatter_dimension=1,
        tiled=True,
    ).astype(jnp.float32)
    flat_grad = hidden_grad.transpose(1, 0, 2).reshape(tok_rows, hid_width)
    gate_grad = (flat_grad * up_val * gate_sig * (1.0 + gate_val * (1.0 - gate_sig))).astype(
        jnp.bfloat16
    )
    up_grad = (flat_grad * silu_val).astype(jnp.bfloat16)
    return (projected, gate_grad, up_grad, tile_grad)


def solution(mesh):
    in_specs = (
        P("dp", "tensor"),
        P("dp", "tensor"),
        P("dp", "tensor"),
        P("tensor", "dp", None, None),
        P("tensor", "dp"),
        P("tensor"),
    )
    out_specs = (
        P("dp", "tensor"),
        P("dp", "tensor"),
        P("dp", "tensor"),
        P("tensor", "dp", None, None),
    )
    return jax.shard_map(
        per_device, mesh=mesh, in_specs=in_specs, out_specs=out_specs, check_vma=False
    )
```

profile of v0, /device:TPU:8, one launch (start us, length us, event | category | flops | bytes accessed | tf_op | source)
XLA Modules:
  0.0 349.0 jit_solution(15729898504732721188)
XLA Ops:
  7.2 0.9 copy.40
  8.2 0.7 copy.41
  9.0 0.7 all-gather.3.cloned.1.call-update
  10.4 1.1 copy.35
  11.5 1.8 copy.36
  13.3 1.3 dynamic-slice
  15.2 0.8 bitcast_dynamic-update-slice_fusion
  15.9 24.1 %all-reduce = s32[96]{0:T(128)S(1)} all-reduce(s32[96]{0:T(128)S(1)} %bitcast_dynamic-update-slice_fusion), channel_id=1, replica_groups=mesh['dp'=32,'tensor'=16] {'dp'}, use_global_device_ids=true, to_apply=%add | all-reduce | flops 96 | bytes 768 | tf_op jit(solution)/shard_map/squeeze | solution.py:28
  40.1 45.9 %all-gather.5.cloned.1.call-done = bf16[32,128,128]{2,1,0:T(8,128)(2,1)} async-done(((bf16[2,128,128]{2,1,0:T(8,128)(2,1)}), bf16[32,128,128]{2,1,0:T(8,128)(2,1)}) %all-gather.5.cloned.1.call-update) | async-done | bytes 1048592 | tf_op jit(solution)/shard_map/all_gather | solution.py:59
  86.0 2.4 gather_fusion.1
  88.4 89.2 %all-gather.3.cloned.1.call-done = bf16[1,96,128,128]{3,2,0,1:T(8,128)(2,1)} async-done(((bf16[1,3,128,128]{3,2,0,1:T(8,128)(2,1)}), bf16[1,96,128,128]{3,2,0,1:T(8,128)(2,1)}) %all-gather.3.cloned.1.call-update) | async-done | bytes 3145744 | tf_op jit(solution)/shard_map/all_gather | solution.py:24
  177.6 6.8 %broadcast_select_fusion = f32[96,128,128]{2,1,0:T(8,128)} fusion(pred[96]{0:T(512)(128)(4,1)S(1)} %iota_compare_fusion, bf16[96,128,128]{2,1,0:T(8,128)(2,1)S(1)} %gather_fusion.1, bf16[1,96,128,128]{3,2,0,1:T(8,128)(2,1)} %all-gather.3.cloned.1.call-done), kind=kOutput, calls=%fused_computation.19 | convolution fusion | flops 404226048 | bytes 12583008 | tf_op jit(solution)/shard_map/gtc,gbc->gtb/dot_general | solution.py:70
  184.5 12.9 %scatter_fusion.1 = f32[7,128,128]{2,1,0:T(8,128)S(1)} fusion(f32[7,128,128]{2,1,0:T(8,128)S(1)} %broadcast_in_dim.84, s32[96]{0:T(128)S(1)} %get-tuple-element.220, f32[96,128,128]{2,1,0:T(8,128)} %broadcast_select_fusion), kind=kCustom, calls=%fused_computation.4 | custom fusion | flops 1572864 | bytes 18874752 | tf_op jit(solution)/shard_map/scatter-add | solution.py:72
  198.1 2.7 gather_fusion.2
  200.8 5.5 %fusion.2 = bf16[1,96,128,128]{3,2,1,0:T(8,128)(2,1)} fusion(pred[96]{0:T(512)(128)(4,1)S(1)} %iota_compare_fusion, bf16[96,128,128]{1,2,0:T(8,128)(2,1)} %gather_fusion.2, bf16[96,128,128]{2,1,0:T(8,128)(2,1)} %copy-done), kind=kOutput, calls=%fused_computation.18 | convolution fusion | flops 407371776 | bytes 9437280 | tf_op jit(solution)/shard_map/gtb,gtc->gbc/dot_general | solution.py:74
  206.3 1.6 broadcast_in_dim.83
  207.9 37.1 %while.15 = (s32[]{:T(128)}, f32[32,128,128]{2,1,0:T(8,128)}, s32[96]{0:T(128)S(1)}, s32[]{:T(128)}, bf16[7,128,128]{2,1,0:T(8,128)(2,1)S(1)}, /*index=5*/bf16[9...) while((s32[]{:T(128)}, f32[32,128,128]{2,1,0:T(8,128)}, s32[96]{0:T(128)S(1)}, ...), condition=%wide.region_2.3_spmd, body=%wide.region_0.2_spmd.sunk | while | flops 67634632 | bytes 6296259 | solution.py:47
  208.0 0.6 gather_fusion
  208.7 0.7 add_compare_fusion.2
  209.3 1.3 convolution_select_fusion.2
  210.7 3.4 scatter_fusion
  214.2 0.6 gather_fusion
  214.8 0.7 add_compare_fusion.2
  215.5 1.3 convolution_select_fusion.2
  216.9 3.4 scatter_fusion
  220.4 0.6 gather_fusion
  221.0 0.7 add_compare_fusion.2
  221.7 1.4 convolution_select_fusion.2
  223.1 3.4 scatter_fusion
  227.3 0.7 add_compare_fusion.2
  227.9 1.3 convolution_select_fusion.2
  229.3 3.4 scatter_fusion
  232.8 0.6 gather_fusion
  233.4 0.7 add_compare_fusion.2
  234.1 1.3 convolution_select_fusion.2
  235.5 3.4 scatter_fusion
  238.9 0.6 gather_fusion
  239.6 0.7 add_compare_fusion.2
  240.2 1.4 convolution_select_fusion.2
  241.6 3.4 scatter_fusion
  245.0 2.8 convert_bitcast_fusion
  247.8 7.3 %all-to-all-start = ((bf16[1,32,128,128]{3,2,0,1:T(8,128)(2,1)}), bf16[1,32,128,128]{3,2,0,1:T(8,128)(2,1)S(1)}, u32[]{:S(2)}, u32[]{:S(2)}) async-start(bf16[1,32,128,128]{3,2,0,1:T(8,128)(2,1)} %convert_bitcast_fusion), calls=%async_computation | async-start | bytes 2097152 | tf_op jit(solution)/shard_map/all_to_all | solution.py:51
  255.0 0.8 copy.44
  255.9 0.8 copy.45
  256.7 25.1 %all-to-all-done = bf16[1,32,128,128]{3,2,0,1:T(8,128)(2,1)S(1)} async-done(((bf16[1,32,128,128]{3,2,0,1:T(8,128)(2,1)}), bf16[1,32,128,128]{3,2,0,1:T(8,128)(2,1)S(1)}, u32[]{:S(2)}, u32[]{:S(2)}) %all-to-all-start) | async-done | bytes 1048608 | tf_op jit(solution)/shard_map/all_to_all | solution.py:51
  282.0 0.7 copy.43
  282.8 58.1 %reduce-scatter.2.cloned.1.call-done = bf16[1,3,128,128]{3,2,1,0:T(8,128)(2,1)} async-done(((bf16[1,96,128,128]{3,2,1,0:T(8,128)(2,1)}), bf16[1,3,128,128]{3,2,1,0:T(8,128)(2,1)}) %reduce-scatter.2.cloned.1.call-update) | async-done | bytes 98320 | tf_op jit(solution)/shard_map/reduce_scatter | solution.py:80
  340.9 1.6 convert_element_type.58
  (39 shorter events, 2.4 us)
Async XLA Ops:
  7.2 78.8 %all-gather.5.cloned.1.call-start = ((), (), s32[]{:S(2)}) async-start(), calls=%async_computation.3 | async-start | bytes 1114112 | tf_op jit(solution)/shard_map/all_gather | solution.py:59
  8.9 168.7 %all-gather.3.cloned.1.call-start = ((), (), s32[]{:S(2)}) async-start(), calls=%async_computation.2 | async-start | bytes 3244032 | tf_op jit(solution)/shard_map/all_gather | solution.py:24
  9.7 331.2 %reduce-scatter.2.cloned.1.call-start = ((), (), s32[]{:S(2)}) async-start(), calls=%async_computation.4 | async-start | bytes 3244032 | tf_op jit(solution)/shard_map/reduce_scatter | solution.py:80
  88.4 89.2 %copy-start = (bf16[96,128,128]{2,1,0:T(8,128)(2,1)}, bf16[96,128,128]{2,1,0:T(8,128)(2,1)S(1)}, u32[]{:S(2)}) copy-start(bf16[96,128,128]{2,1,0:T(8,128)(2,1)S(1)} %gather_fusion.1) | copy-start | bytes 9437188
  184.5 13.1 %copy-start.1 = (bf16[128,896]{0,1:T(8,128)(2,1)S(1)}, bf16[128,896]{0,1:T(8,128)(2,1)}, u32[]{:S(2)}) copy-start(bf16[128,896]{0,1:T(8,128)(2,1)} %copy.36) | copy-start | bytes 688132
  247.8 34.0 %all-to-all-start = ((bf16[1,32,128,128]{3,2,0,1:T(8,128)(2,1)}), bf16[1,32,128,128]{3,2,0,1:T(8,128)(2,1)S(1)}, u32[]{:S(2)}, u32[]{:S(2)}) async-start(bf16[1,32,128,128]{3,2,0,1:T(8,128)(2,1)} %convert_bitcast_fusion), calls=%async_computation | async-start | bytes 2097152 | tf_op jit(solution)/shard_map/all_to_all | solution.py:51
Sparse Core Ops, SparseCore 0:
  10.7 75.2 all-gather.4
  89.4 88.2 all-gather.2
  206.4 134.4 reduce-scatter.1
where the time goes:
time: 350 us; the launch traced here: 349 us
  waiting for transfers between devices  219 us (63%)
  other arithmetic  42.6 us (12%)
  blocking collectives  24.1 us (7%)
  matrix products  20.4 us (6%)
  local copies, waits for them, and re-layouts  20.1 us (6%)
  between operations  15.2 us (4%)
  starting transfers between devices  7.4 us (2%)
    all_gather x1, waiting for transfers between devices, per_device(): lax.all_gather(weight_tiles, 'dp', axis=1, tiled=True)  89.2 us
    reduce_scatter x1, waiting for transfers between devices, per_device(): lax.psum_scatter(grad_buffer.reshape(1, capacity, tile_edge, tile_edge).a...  58.1 us
    all_gather x1, waiting for transfers between devices, per_device(): all_cot = lax.all_gather(cot_local, 'tensor', axis=0, tiled=True)  45.9 us
    all_to_all x1, waiting for transfers between devices, per_device(): lax.all_to_all(shared, 'tensor', split_axis=1, concat_axis=0, tiled=True)  25.1 us
    squeeze x1, blocking collectives, per_device(): all_slots = fetched_slots[0]  24.1 us
    scatter-add x6, other arithmetic, forward_group(): return totals.at[mod_index].add(product)  20.4 us
    scatter-add x1, other arithmetic, per_device(): hidden_grad = hidden_grad.at[hid_index].add(back)  12.9 us
    unnamed x13, local copies, waits for them, and re-layouts  8.27 us
  transfers between devices with their start and end apart: 4, of which 4 were waited for; matrix products, arithmetic and copies ran while one was open for 15% of the time, Pallas kernels for 0%

commit v1 on v0

--- a/solution.py
+++ b/solution.py
@@ -56,7 +56,16 @@
         .astype(jnp.bfloat16)
     )
     cot_local = cotangent.reshape(tok_rows, local_blocks, tile_edge).transpose(1, 0, 2)
-    all_cot = lax.all_gather(cot_local, "tensor", axis=0, tiled=True)
+    time_marks = lambda frame, which_dim: jnp.concatenate(
+        lax.all_to_all(
+            jnp.stack([frame for _ in range(lax.psum(1, axis_name="tensor"))], 0),
+            "tensor",
+            split_axis=0,
+            concat_axis=0,
+        ),
+        which_dim,
+    )
+    all_cot = time_marks(cot_local, 0)
     part_tiles = lax.all_gather(weight_tiles, "dp", axis=1, tiled=True)[0]
     part_slots = lax.all_gather(tile_slots, "dp", axis=1, tiled=True)[0]
     hidden_grad = jnp.zeros((hid_blocks, tok_rows, tile_edge), jnp.float32)

time: 350 us -> 281 us (0.80)
  waiting for transfers between devices: 219 us -> 143 us
  starting transfers between devices: 7.4 us -> 16.6 us
    all_gather x1 -> x0, waiting for transfers between devices: 45.9 us -> none  [per_device(): all_cot = lax.all_gather(cot_local, 'tensor', axis=0, tiled=True)]
    all_gather x1, waiting for transfers between devices: 89.2 us -> 59.1 us  [per_device(): lax.all_gather(weight_tiles, 'dp', axis=1, tiled=True)]
    all_to_all x0 -> x1, starting transfers between devices: none -> 9.26 us  [per_device(): lax.all_to_all(jnp.stack([frame for _ in range(lax.psum(1, axis_name='ten...]
    unnamed x13 -> x14, local copies, waits for them, and re-layouts: 8.27 us -> 4.15 us
  transfers between devices with their start and end apart: 4 -> 4, of which waited for: 4 -> 3; matrix products, arithmetic and copies ran while one was open for 15% -> 18% of each run, Pallas kernels for 0% -> 0%
where the time goes in v1:
time: 281 us; the launch traced here: 280 us
  waiting for transfers between devices  143 us (51%)
  other arithmetic  42.7 us (15%)
  blocking collectives  23.1 us (8%)
  matrix products  21.4 us (8%)
  local copies, waits for them, and re-layouts  17.6 us (6%)
  starting transfers between devices  16.6 us (6%)
  between operations  15.5 us (6%)
    all_gather x1, waiting for transfers between devices, per_device(): lax.all_gather(weight_tiles, 'dp', axis=1, tiled=True)  59.1 us
    reduce_scatter x1, waiting for transfers between devices, per_device(): lax.psum_scatter(grad_buffer.reshape(1, capacity, tile_edge, tile_edge).a...  58.2 us
    all_to_all x1, waiting for transfers between devices, per_device(): lax.all_to_all(shared, 'tensor', split_axis=1, concat_axis=0, tiled=True)  25.1 us
    squeeze x1, blocking collectives, per_device(): all_slots = fetched_slots[0]  23.1 us
    scatter-add x6, other arithmetic, forward_group(): return totals.at[mod_index].add(product)  20.4 us
    scatter-add x1, other arithmetic, per_device(): hidden_grad = hidden_grad.at[hid_index].add(back)  12.9 us
    all_to_all x1, starting transfers between devices, per_device(): lax.all_to_all(jnp.stack([frame for _ in range(lax.psum(1, axis_name='ten...  9.26 us
    dot_general x6, matrix products, forward_group(): jnp.einsum('gtb,gbc->gtc', picked, group_tiles, preferred_element_type=jn...  8.08 us
  transfers between devices with their start and end apart: 4, of which 3 were waited for; matrix products, arithmetic and copies ran while one was open for 18% of the time, Pallas kernels for 0%

profile of v1, /device:TPU:8, one launch (start us, length us, event | category | flops | bytes accessed | tf_op | source)
XLA Modules:
  0.0 280.1 jit_solution(7043800576689017682)
XLA Ops:
  7.2 0.7 all-gather.2.cloned.1.call-update
  7.9 0.9 reshape.165
  8.8 1.2 stack.2
  10.0 9.3 %all-to-all-start.1 = ((bf16[16,2,128,128]{3,2,1,0:T(8,128)(2,1)}), bf16[16,2,128,128]{3,2,1,0:T(8,128)(2,1)S(1)}, u32[]{:S(2)}, u32[]{:S(2)}) async-start(bf16[16,2,128,128]{3,2,1,0:T(8,128)(2,1)} %stack.2), calls=%async_computation.1 | async-start | bytes 2097152 | tf_op jit(solution)/shard_map/all_to_all | solution.py:60
  20.4 1.3 dynamic-slice
  22.4 23.1 %all-reduce = s32[96]{0:T(128)S(1)} all-reduce(s32[96]{0:T(128)S(1)} %bitcast_dynamic-update-slice_fusion), channel_id=1, replica_groups=mesh['dp'=32,'tensor'=16] {'dp'}, use_global_device_ids=true, to_apply=%add | all-reduce | flops 96 | bytes 768 | tf_op jit(solution)/shard_map/squeeze | solution.py:28
  45.5 2.7 gather_fusion.1
  48.2 59.1 %all-gather.2.cloned.1.call-done = bf16[1,96,128,128]{3,2,0,1:T(8,128)(2,1)} async-done(((bf16[1,3,128,128]{3,2,0,1:T(8,128)(2,1)}), bf16[1,96,128,128]{3,2,0,1:T(8,128)(2,1)}) %all-gather.2.cloned.1.call-update) | async-done | bytes 3145744 | tf_op jit(solution)/shard_map/all_gather | solution.py:24
  107.4 7.8 %broadcast_select_fusion = f32[96,128,128]{2,1,0:T(8,128)} fusion(pred[96]{0:T(512)(128)(4,1)S(1)} %iota_compare_fusion, bf16[96,128,128]{2,1,0:T(8,128)(2,1)} %gather_fusion.1, bf16[1,96,128,128]{3,2,0,1:T(8,128)(2,1)} %all-gather.2.cloned.1.call-done), kind=kOutput, calls=%fused_computation.19 | convolution fusion | flops 404226048 | bytes 12583008 | tf_op jit(solution)/shard_map/gtc,gbc->gtb/dot_general | solution.py:79
  115.2 12.9 %scatter_fusion.1 = f32[7,128,128]{2,1,0:T(8,128)S(1)} fusion(f32[7,128,128]{2,1,0:T(8,128)S(1)} %broadcast_in_dim.84, s32[96]{0:T(128)S(1)} %get-tuple-element.210, f32[96,128,128]{2,1,0:T(8,128)} %broadcast_select_fusion), kind=kCustom, calls=%fused_computation.4 | custom fusion | flops 1572864 | bytes 18874752 | tf_op jit(solution)/shard_map/scatter-add | solution.py:81
  128.1 0.2 copy.34
  128.3 0.3 fusion.11
  128.8 2.7 gather_fusion.2
  131.5 5.5 %fusion.2 = bf16[1,96,128,128]{3,2,1,0:T(8,128)(2,1)} fusion(pred[96]{0:T(512)(128)(4,1)S(1)} %iota_compare_fusion, bf16[96,128,128]{1,2,0:T(8,128)(2,1)} %gather_fusion.2, bf16[96,128,128]{2,1,0:T(8,128)(2,1)} %gather_fusion.1), kind=kOutput, calls=%fused_computation.18 | convolution fusion | flops 407371776 | bytes 9437280 | tf_op jit(solution)/shard_map/gtb,gtc->gbc/dot_general | solution.py:83
  137.0 1.6 broadcast_in_dim.83
  138.6 37.1 %while.15 = (s32[]{:T(128)}, f32[32,128,128]{2,1,0:T(8,128)}, s32[96]{0:T(128)S(1)}, s32[]{:T(128)}, bf16[7,128,128]{2,1,0:T(8,128)(2,1)S(1)}, /*index=5*/bf16[9...) while((s32[]{:T(128)}, f32[32,128,128]{2,1,0:T(8,128)}, s32[96]{0:T(128)S(1)}, ...), condition=%wide.region_2.3_spmd, body=%wide.region_0.2_spmd.sunk | while | flops 67634632 | bytes 6296259 | solution.py:47
  138.7 0.6 gather_fusion
  139.3 0.7 add_compare_fusion.2
  140.0 1.3 convolution_select_fusion.2
  141.4 3.4 %scatter_fusion = f32[32,128,128]{2,1,0:T(8,128)} fusion(f32[32,128,128]{2,1,0:T(8,128)} %get-tuple-element.263, s32[16]{0:T(128)S(1)} %compare_select_fusion.14, f32[16,128,128]{2,1,0:T(8,128)S(1)} %convolution_select_fusion.2), kind=kCustom, calls=%fused_computation.3.clone.1 | custom fusion | flops 262144 | bytes 3145792 | tf_op jit(solution)/shard_map/while/body/eval_jaxpr/scatter-add | solution.py:45
  144.9 0.6 gather_fusion
  145.5 0.7 add_compare_fusion.2
  146.2 1.3 convolution_select_fusion.2
  147.5 3.4 %scatter_fusion = f32[32,128,128]{2,1,0:T(8,128)} fusion(f32[32,128,128]{2,1,0:T(8,128)} %get-tuple-element.263, s32[16]{0:T(128)S(1)} %compare_select_fusion.14, f32[16,128,128]{2,1,0:T(8,128)S(1)} %convolution_select_fusion.2), kind=kCustom, calls=%fused_computation.3.clone.1 | custom fusion | flops 262144 | bytes 3145792 | tf_op jit(solution)/shard_map/while/body/eval_jaxpr/scatter-add | solution.py:45
  151.1 0.6 gather_fusion
  151.7 0.7 add_compare_fusion.2
  152.4 1.4 convolution_select_fusion.2
  153.8 3.4 %scatter_fusion = f32[32,128,128]{2,1,0:T(8,128)} fusion(f32[32,128,128]{2,1,0:T(8,128)} %get-tuple-element.263, s32[16]{0:T(128)S(1)} %compare_select_fusion.14, f32[16,128,128]{2,1,0:T(8,128)S(1)} %convolution_select_fusion.2), kind=kCustom, calls=%fused_computation.3.clone.1 | custom fusion | flops 262144 | bytes 3145792 | tf_op jit(solution)/shard_map/while/body/eval_jaxpr/scatter-add | solution.py:45
  157.3 0.6 gather_fusion
  157.9 0.7 add_compare_fusion.2
  158.6 1.3 convolution_select_fusion.2
  160.0 3.4 %scatter_fusion = f32[32,128,128]{2,1,0:T(8,128)} fusion(f32[32,128,128]{2,1,0:T(8,128)} %get-tuple-element.263, s32[16]{0:T(128)S(1)} %compare_select_fusion.14, f32[16,128,128]{2,1,0:T(8,128)S(1)} %convolution_select_fusion.2), kind=kCustom, calls=%fused_computation.3.clone.1 | custom fusion | flops 262144 | bytes 3145792 | tf_op jit(solution)/shard_map/while/body/eval_jaxpr/scatter-add | solution.py:45
  163.5 0.6 gather_fusion
  164.1 0.7 add_compare_fusion.2
  164.8 1.3 convolution_select_fusion.2
  166.1 3.4 %scatter_fusion = f32[32,128,128]{2,1,0:T(8,128)} fusion(f32[32,128,128]{2,1,0:T(8,128)} %get-tuple-element.263, s32[16]{0:T(128)S(1)} %compare_select_fusion.14, f32[16,128,128]{2,1,0:T(8,128)S(1)} %convolution_select_fusion.2), kind=kCustom, calls=%fused_computation.3.clone.1 | custom fusion | flops 262144 | bytes 3145792 | tf_op jit(solution)/shard_map/while/body/eval_jaxpr/scatter-add | solution.py:45
  169.6 0.6 gather_fusion
  170.3 0.7 add_compare_fusion.2
  170.9 1.4 convolution_select_fusion.2
  172.3 3.4 %scatter_fusion = f32[32,128,128]{2,1,0:T(8,128)} fusion(f32[32,128,128]{2,1,0:T(8,128)} %get-tuple-element.263, s32[16]{0:T(128)S(1)} %compare_select_fusion.14, f32[16,128,128]{2,1,0:T(8,128)S(1)} %convolution_select_fusion.2), kind=kCustom, calls=%fused_computation.3.clone.1 | custom fusion | flops 262144 | bytes 3145792 | tf_op jit(solution)/shard_map/while/body/eval_jaxpr/scatter-add | solution.py:45
  175.7 2.8 convert_bitcast_fusion
  178.4 7.3 %all-to-all-start = ((bf16[1,32,128,128]{3,2,0,1:T(8,128)(2,1)}), bf16[1,32,128,128]{3,2,0,1:T(8,128)(2,1)S(1)}, u32[]{:S(2)}, u32[]{:S(2)}) async-start(bf16[1,32,128,128]{3,2,0,1:T(8,128)(2,1)} %convert_bitcast_fusion), calls=%async_computation | async-start | bytes 2097152 | tf_op jit(solution)/shard_map/all_to_all | solution.py:51
  185.7 0.8 copy.36
  186.5 0.8 copy.37
  187.4 25.1 %all-to-all-done = bf16[1,32,128,128]{3,2,0,1:T(8,128)(2,1)S(1)} async-done(((bf16[1,32,128,128]{3,2,0,1:T(8,128)(2,1)}), bf16[1,32,128,128]{3,2,0,1:T(8,128)(2,1)S(1)}, u32[]{:S(2)}, u32[]{:S(2)}) %all-to-all-start) | async-done | bytes 1048608 | tf_op jit(solution)/shard_map/all_to_all | solution.py:51
  212.7 0.7 copy.35
  213.5 58.2 %reduce-scatter.2.cloned.1.call-done = bf16[1,3,128,128]{3,2,1,0:T(8,128)(2,1)} async-done(((bf16[1,96,128,128]{3,2,1,0:T(8,128)(2,1)}), bf16[1,3,128,128]{3,2,1,0:T(8,128)(2,1)}) %reduce-scatter.2.cloned.1.call-update) | async-done | bytes 98320 | tf_op jit(solution)/shard_map/reduce_scatter | solution.py:89
  271.6 1.6 convert_element_type.58
  (41 shorter events, 1.7 us)
Async XLA Ops:
  7.2 12.8 %copy-start = (bf16[128,896]{1,0:T(8,128)(2,1)S(1)}, bf16[128,896]{1,0:T(8,128)(2,1)}, u32[]{:S(2)}) copy-start(bf16[128,896]{1,0:T(8,128)(2,1)} %param.8) | copy-start | bytes 688132
  7.2 13.0 %copy-start.1 = (bf16[128,896]{1,0:T(8,128)(2,1)S(1)}, bf16[128,896]{1,0:T(8,128)(2,1)}, u32[]{:S(2)}) copy-start(bf16[128,896]{1,0:T(8,128)(2,1)} %param.9) | copy-start | bytes 688132
  7.2 15.1 %copy-start.2 = (s32[1,3]{1,0:T(1,128)S(1)}, s32[1,3]{1,0:T(1,128)}, u32[]{:S(2)}) copy-start(s32[1,3]{1,0:T(1,128)} %param.12) | copy-start | bytes 40
  7.2 100.2 %all-gather.2.cloned.1.call-start = ((), (), s32[]{:S(2)}) async-start(), calls=%async_computation.3 | async-start | bytes 3244032 | tf_op jit(solution)/shard_map/all_gather | solution.py:24
  10.0 35.5 %all-to-all-start.1 = ((bf16[16,2,128,128]{3,2,1,0:T(8,128)(2,1)}), bf16[16,2,128,128]{3,2,1,0:T(8,128)(2,1)S(1)}, u32[]{:S(2)}, u32[]{:S(2)}) async-start(bf16[16,2,128,128]{3,2,1,0:T(8,128)(2,1)} %stack.2), calls=%async_computation.1 | async-start | bytes 2097152 | tf_op jit(solution)/shard_map/all_to_all | solution.py:60
  19.3 252.4 %reduce-scatter.2.cloned.1.call-start = ((), (), s32[]{:S(2)}) async-start(), calls=%async_computation.4 | async-start | bytes 3244032 | tf_op jit(solution)/shard_map/reduce_scatter | solution.py:89
  178.4 34.0 %all-to-all-start = ((bf16[1,32,128,128]{3,2,0,1:T(8,128)(2,1)}), bf16[1,32,128,128]{3,2,0,1:T(8,128)(2,1)S(1)}, u32[]{:S(2)}, u32[]{:S(2)}) async-start(bf16[1,32,128,128]{3,2,0,1:T(8,128)(2,1)} %convert_bitcast_fusion), calls=%async_computation | async-start | bytes 2097152 | tf_op jit(solution)/shard_map/all_to_all | solution.py:51
Sparse Core Ops, SparseCore 0:
  11.4 95.9 all-gather.1
  137.1 134.4 reduce-scatter.1
